TPU v7x, 32 devices: a whole 2x2x4 slice. The times are simulated.
32 devices in a mesh: groups: 2 (over y), vox: 4 (over z), freq: 2 (over x), sub: 2 (over core).
Axes of the slice: x: 2, y: 2, z: 4, core: 2. Of those that a mesh axis runs over, the one named last changes fastest.
Arguments:
- residual: bfloat16 [4, 1024, 1024], P(('groups', 'freq'), 'vox', 'sub'), parts along dimension 0, may hold values from -6 to 6
- green: bfloat16 [4, 1024, 8192], P(('groups', 'freq'), None, 'vox'), parts along dimension 0, may hold values from -0.15625 to 0.15625
- active: int32 [4, 1024], P(('groups', 'freq')), parts along dimension 0, may hold values 0 or 1
- aperture: int32 [4], P(('groups', 'freq')), parts along dimension 0, may hold values from 256 to 511
- step_gain: float32 [4], P(('groups', 'freq')), parts along dimension 0, may hold values from 6 to 24
- block_region: int32 [128], P(('groups', 'vox')), parts along dimension 0, may hold values from 0 to 15
- strength: float32 [16], replicated, may hold values from 0.1 to 1
Outputs:
- updated: float32 [4, 1024, 1024], P(('groups', 'freq'), 'vox', 'sub'), parts along dimension 0
There are 2 independent parts, one for each index of `groups`. A program takes and returns all parts, laid end to end along the dimension named above; an argument that names none is the same for every part. Nothing has to cross between parts.
All inputs are finite; a program needn't handle non-finite values. No bound on the sum of `active` on one device may be relied on, other than what follows from the above.
Results may differ from a plain program's by a relative error of at most 0.0026.
Values may be sent and summed in bfloat16 or wider, within the bound.
No kernel may reach another device: no remote copies, remote signals or barrier semaphores. Data moves between devices by JAX's collectives and lax.ppermute only.
A program may use at most 64 MiB of HBM per device.

v0:
```python
import jax
import jax.numpy as jnp
from jax import lax
from jax.sharding import PartitionSpec as P

BLOCK = 128
REGIONS = 16


smooth_sq = 0.0625


def penalize(image_sum, strength_map):
    return image_sum - strength_map * image_sum / jnp.sqrt(image_sum * image_sum + smooth_sq)


def body(residual, green, active, aperture, step_gain, block_region, strength):
    local_data = residual[0]
    green_rows = green[0]
    element_on = active[0]
    rows_local = local_data.shape[0]
    cols_local = local_data.shape[1]
    row_start = lax.axis_index("vox") * rows_local
    col_start = lax.axis_index("sub") * cols_local
    row_ids = row_start + jnp.arange(rows_local, dtype=jnp.int32)
    col_ids = col_start + jnp.arange(cols_local, dtype=jnp.int32)
    row_on = lax.dynamic_slice_in_dim(element_on, row_start, rows_local)
    col_on = lax.dynamic_slice_in_dim(element_on, col_start, cols_local)
    in_band = (jnp.abs(row_ids[:, None] - col_ids[None, :]) <= aperture[0]).astype(jnp.int32)
    pair_mask = row_on[:, None] * col_on[None, :] * in_band
    masked = local_data * pair_mask.astype(jnp.bfloat16)
    tx_green = lax.dynamic_slice_in_dim(green_rows, col_start, cols_local, 0)
    rx_green = green_rows
    beamed = lax.dot_general(
        lax.all_gather(masked, "vox", axis=0, tiled=True),
        rx_green,
        (((0,), (0,)), ((), ())),
        preferred_element_type=jnp.float32,
    )
    partial_value = jnp.sum(tx_green.astype(jnp.float32) * beamed, axis=0)
    region_ids = jnp.arange(REGIONS, dtype=jnp.int32)
    onehot = (block_region[:, None] == region_ids[None, :]).astype(jnp.float32)
    block_strength = jnp.dot(onehot, strength, precision=lax.Precision.HIGHEST)
    strength_map = jnp.broadcast_to(
        block_strength[:, None], (block_region.shape[0], BLOCK)
    ).reshape(-1)
    image_sum = lax.psum(partial_value, ("freq", "sub"))
    scaled = penalize(image_sum, strength_map)
    weighted = (tx_green.astype(jnp.float32) * scaled[None, :]).astype(jnp.bfloat16)
    rx_green = green_rows
    gradient = lax.psum_scatter(
        lax.dot_general(
            rx_green, weighted, (((1,), (1,)), ((), ())), preferred_element_type=jnp.float32
        ),
        "vox",
        scatter_dimension=0,
        tiled=True,
    )
    updated = pair_mask.astype(jnp.float32) * (
        local_data.astype(jnp.float32) - step_gain[0] * gradient
    )
    return updated[None]


def solution(mesh):
    in_specs = (
        P(("groups", "freq"), "vox", "sub"),
        P(("groups", "freq"), None, "vox"),
        P(("groups", "freq"), None),
        P(("groups", "freq")),
        P(("groups", "freq")),
        P(("groups", "vox")),
        P(),
    )
    out_specs = P(("groups", "freq"), "vox", "sub")
    return jax.shard_map(body, mesh=mesh, in_specs=in_specs, out_specs=out_specs, check_vma=False)
```

profile of v0, /device:TPU:0, one launch (start us, length us, event | category | flops | bytes accessed | tf_op | source)
XLA Modules:
  0.0 112.5 jit_solution(282476886270664636)
XLA Ops:
  6.5 0.0 copy-start
  6.5 0.0 all-gather.2.cloned.1.call-start
  6.5 0.7 copy-done
  7.2 1.1 copy.8
  9.0 1.0 fusion.19
  9.9 0.0 all-gather.2.cloned.1.call-update
  9.9 0.0 reduce-scatter.2.cloned.1.call-start
  10.0 0.9 convolution_bitcast_fusion
  10.9 32.1 %all-gather.2.cloned.1.call-done = bf16[1024,512]{0,1:T(8,128)(2,1)} async-done(((bf16[256,512]{0,1:T(8,128)(2,1)}), bf16[1024,512]{0,1:T(8,128)(2,1)}) %all-gather.2.cloned.1.call-update) | async-done | bytes 1048592 | tf_op jit(solution)/shard_map/all_gather | solution.py:35
  43.0 5.5 %fusion.2 = f32[2048]{0:T(1024)S(1)} fusion(bf16[1,1024,2048]{2,1,0:T(8,128)(2,1)} %param.8, s32[]{:T(128)S(6)} %select_n.8, bf16[1024,512]{0,1:T(8,128)(2,1)} %all-gather.2.cloned.1.call-done), kind=kOutput, calls=%fused_computation.4 | convolution fusion | flops 2150627328 | bytes 7348228 | tf_op jit(solution)/shard_map/dot_general | solution.py:34
  48.5 5.9 %psum.7 = f32[2048]{0:T(1024)S(1)} all-reduce(f32[2048]{0:T(1024)S(1)} %fusion.2), channel_id=1, replica_groups=mesh['groups'=2,'vox'=4,'freq'=2,'sub'=2] {'freq','sub'}, use_global_device_ids=true, to_apply=%region_1.0 | all-reduce | flops 2048 | bytes 16384 | tf_op jit(solution)/shard_map/psum | solution.py:47
  54.5 0.1 fusion.21
  54.5 6.5 %fusion.11 = f32[1024,512]{0,1:T(8,128)} fusion(bf16[1,1024,2048]{2,1,0:T(8,128)(2,1)} %param.8, f32[2048]{0:T(1024)S(1)} %fusion.21, s32[]{:T(128)S(6)} %select_n.8), kind=kOutput, calls=%fused_computation.12 | convolution fusion | flops 2150629376 | bytes 8396804 | tf_op jit(solution)/shard_map/dot_general | solution.py:52
  61.1 0.0 reduce-scatter.2.cloned.1.call-update
  61.8 41.6 %reduce-scatter.2.cloned.1.call-done = f32[256,512]{0,1:T(8,128)} async-done(((f32[1024,512]{0,1:T(8,128)}), f32[256,512]{0,1:T(8,128)}) %reduce-scatter.2.cloned.1.call-update) | async-done | bytes 524304 | tf_op jit(solution)/shard_map/reduce_scatter | solution.py:51
  103.4 1.3 %multiply_bitcast_fusion = f32[1,256,512]{1,2,0:T(8,128)S(1)} fusion(f32[256,512]{0,1:T(8,128)} %reduce-scatter.2.cloned.1.call-done, bf16[1,256,512]{1,2,0:T(8,128)(2,1)S(1)} %copy.8, f32[]{:T(128)} %bitcast.45, s32[512]{0:T(512)S(1)} %bitcast.47, s32[256]{0:T(256)S(1)} %bitcast.49, s32[]{:T(128)} %bitcast.43, s32[512]{0:T(512)S(1)} %iota_add_fusion, ...), kind=kLoop, calls=%fused_computation.14 | loop fusion | flops 1310720 | bytes 1316872 | tf_op jit(solution)/shard_map/broadcast_in_dim | solution.py:62
  104.7 1.0 copy.9
  (4 shorter events, 0.0 us)
Async XLA Ops:
  6.5 0.7 copy-start
  6.5 36.5 %all-gather.2.cloned.1.call-start = ((), (), s32[]{:S(2)}) async-start(), calls=%async_computation.1 | async-start | bytes 1310720 | tf_op jit(solution)/shard_map/all_gather | solution.py:35
  9.9 93.4 %reduce-scatter.2.cloned.1.call-start = ((), (), s32[]{:S(2)}) async-start(), calls=%async_computation.2 | async-start | bytes 2621440 | tf_op jit(solution)/shard_map/reduce_scatter | solution.py:51
Sparse Core Ops, SparseCore 0:
  10.1 32.8 all-gather.1
  61.2 42.0 reduce-scatter.1
where the time goes:
time: 113 us
  waiting for transfers between devices  73.8 us (65%)
  between operations  14.7 us (13%)
  matrix products  12.9 us (11%)
  blocking collectives  5.94 us (5%)
  local copies, waits for them, and re-layouts  2.75 us (2%)
  other arithmetic  2.33 us (2%)
    reduce_scatter x1, waiting for transfers between devices, body(): lax.psum_scatter(lax.dot_general(rx_green, weighted, (((1,), (1,)), ((),...  41.6 us
    all_gather x1, waiting for transfers between devices, body(): lax.all_gather(masked, 'vox', axis=0, tiled=True)  32.1 us
    dot_general x1, matrix products, body(): lax.dot_general(rx_green, weighted, (((1,), (1,)), ((), ())), preferred_e...  6.55 us
    psum x1, blocking collectives, body(): image_sum = lax.psum(partial_value, ('freq', 'sub'))  5.94 us
    dot_general x1, matrix products, body(): lax.dot_general(lax.all_gather(masked, 'vox', axis=0, tiled=True), rx_gre...  5.52 us
  transfers between devices with their start and end apart: 2, of which 2 were waited for; matrix products, arithmetic and copies ran while one was open for 1% of the time, Pallas kernels for 0%

commit v1 on v0

v1 whole, which is shorter than its diff:
```python
import jax
import jax.numpy as jnp
from jax import lax
from jax.sharding import PartitionSpec as P

BLOCK = 128
REGIONS = 16


smooth_sq = 0.0625


def penalize(image_sum, strength_map):
    return image_sum - strength_map * image_sum / jnp.sqrt(image_sum * image_sum + smooth_sq)


def rotation(count, step):
    return [(i, (i + step) % count) for i in range(count)]


def body(sizes, residual, green, active, aperture, step_gain, block_region, strength):
    vox_n = sizes["vox"]
    local_data = residual[0]
    green_rows = green[0]
    element_on = active[0]
    rows_local = local_data.shape[0]
    cols_local = local_data.shape[1]
    me = lax.axis_index("vox")
    row_start = me * rows_local
    col_start = lax.axis_index("sub") * cols_local
    row_ids = row_start + jnp.arange(rows_local, dtype=jnp.int32)
    col_ids = col_start + jnp.arange(cols_local, dtype=jnp.int32)
    row_on = lax.dynamic_slice_in_dim(element_on, row_start, rows_local)
    col_on = lax.dynamic_slice_in_dim(element_on, col_start, cols_local)
    in_band = (jnp.abs(row_ids[:, None] - col_ids[None, :]) <= aperture[0]).astype(jnp.int32)
    pair_mask = row_on[:, None] * col_on[None, :] * in_band
    masked = local_data * pair_mask.astype(jnp.bfloat16)
    tx_green = lax.dynamic_slice_in_dim(green_rows, col_start, cols_local, 0)

    def rows_of(array, owner):
        return lax.dynamic_slice_in_dim(array, owner * rows_local, rows_local, 0)

    gathered = jnp.zeros((vox_n * rows_local, cols_local), masked.dtype)
    for step in range(vox_n):
        piece = masked if step == 0 else lax.ppermute(masked, "vox", rotation(vox_n, step))
        gathered = lax.dynamic_update_slice_in_dim(
            gathered, piece, (me - step) % vox_n * rows_local, 0
        )
    beamed = lax.dot_general(
        gathered, green_rows, (((0,), (0,)), ((), ())), preferred_element_type=jnp.float32
    )
    image_sum = jnp.sum(tx_green.astype(jnp.float32) * beamed, axis=0).reshape(-1, BLOCK)
    region_ids = jnp.arange(REGIONS, dtype=jnp.int32)
    onehot = (block_region[:, None] == region_ids[None, :]).astype(jnp.float32)
    block_strength = jnp.dot(onehot, strength, precision=lax.Precision.HIGHEST)
    for axis in ("sub", "freq"):
        count = sizes[axis]
        own = image_sum
        for step in range(1, count):
            image_sum = image_sum + lax.ppermute(own, axis, rotation(count, step))
    scaled = penalize(image_sum, block_strength[:, None]).reshape(-1)
    weighted = (tx_green.astype(jnp.float32) * scaled[None, :]).astype(jnp.bfloat16)
    gradient = lax.dot_general(
        green_rows, weighted, (((1,), (1,)), ((), ())), preferred_element_type=jnp.float32
    )
    sendable = gradient.astype(jnp.bfloat16)
    total = rows_of(gradient, me)
    for step in range(1, vox_n):
        piece = rows_of(sendable, (me + step) % vox_n)
        total = total + lax.ppermute(piece, "vox", rotation(vox_n, step)).astype(jnp.float32)
    updated = pair_mask.astype(jnp.float32) * (
        local_data.astype(jnp.float32) - step_gain[0] * total
    )
    return updated[None]


def solution(mesh):
    sizes = dict(mesh.shape)
    in_specs = (
        P(("groups", "freq"), "vox", "sub"),
        P(("groups", "freq"), None, "vox"),
        P(("groups", "freq"), None),
        P(("groups", "freq")),
        P(("groups", "freq")),
        P(("groups", "vox")),
        P(),
    )
    out_specs = P(("groups", "freq"), "vox", "sub")

    def local(*arrays):
        return body(sizes, *arrays)

    return jax.shard_map(local, mesh=mesh, in_specs=in_specs, out_specs=out_specs, check_vma=False)
```

time: 113 us -> 70 us (0.62)
  the two profiles are of different devices: /device:TPU:0 before, /device:TPU:11 now
where the time goes in v1:
time: 70 us; the launch traced here: 69.8 us
  waiting for transfers between devices  46.6 us (67%)
  matrix products  10.6 us (15%)
  starting transfers between devices  7.51 us (11%)
  local copies, waits for them, and re-layouts  3.06 us (4%)
  between operations  1.43 us (2%)
    ppermute x3, waiting for transfers between devices, body(): lax.ppermute(masked, 'vox', rotation(vox_n, step))  22.1 us
    ppermute x3, waiting for transfers between devices, body(): lax.ppermute(piece, 'vox', rotation(vox_n, step)).astype(jnp.float32)  21.5 us
    dot_general x1, matrix products, body(): lax.dot_general(gathered, green_rows, (((0,), (0,)), ((), ())), preferred...  5.25 us
    dot_general x1, matrix products, body(): lax.dot_general(green_rows, weighted, (((1,), (1,)), ((), ())), preferred...  5.19 us
    ppermute x3, starting transfers between devices, body(): lax.ppermute(masked, 'vox', rotation(vox_n, step))  3.83 us
    ppermute x2, waiting for transfers between devices, body(): image_sum = image_sum + lax.ppermute(own, axis, rotation(count, step))  2.88 us
    ppermute x3, starting transfers between devices, body(): lax.ppermute(piece, 'vox', rotation(vox_n, step)).astype(jnp.float32)  2.87 us
    unnamed x7, local copies, waits for them, and re-layouts  1.76 us
  transfers between devices with their start and end apart: 8, of which 8 were waited for; matrix products, arithmetic and copies ran while one was open for 0% of the time, Pallas kernels for 0%

profile of v1, /device:TPU:11, one launch (start us, length us, event | category | flops | bytes accessed | tf_op | source)
XLA Modules:
  0.0 69.8 jit_solution(16525223532861825083)
XLA Ops:
  0.0 0.0 copy-start
  0.0 0.7 copy-done
  0.7 1.1 %copy.8 = bf16[1,256,512]{1,2,0:T(8,128)(2,1)S(1)} copy(bf16[1,256,512]{2,1,0:T(8,128)(2,1)} %param.7) | data formatting | bytes 524288 | tf_op args[0]
  2.4 0.1 broadcast_in_dim.4
  2.6 0.3 constant_dynamic-update-slice_fusion.3
  2.8 1.3 %collective-permute-start = (bf16[256,512]{0,1:T(8,128)(2,1)S(1)}, bf16[256,512]{0,1:T(8,128)(2,1)S(1)}, u32[]{:S(2)}, u32[]{:S(2)}) collective-permute-start(bf16[256,512]{0,1:T(8,128)(2,1)S(1)} %get-tuple-element.6), channel_id=1, source_target_pairs={{0,4},{4,8},{8,12},{12,0},{1,5},{5,9},{9,13},{13,1},{2,6},{6,10},{... | collective-permute-start | bytes 786440 | tf_op jit(solution)/shard_map/ppermute | solution.py:45
  4.2 1.1 %collective-permute-start.1 = (bf16[256,512]{0,1:T(8,128)(2,1)S(1)}, bf16[256,512]{0,1:T(8,128)(2,1)S(1)}, u32[]{:S(2)}, u32[]{:S(2)}) collective-permute-start(bf16[256,512]{0,1:T(8,128)(2,1)S(1)} %get-tuple-element.6), channel_id=1, source_target_pairs={{0,8},{4,12},{8,0},{12,4},{1,9},{5,13},{9,1},{13,5},{2,10},{6,14},... | collective-permute-start | bytes 786440 | tf_op jit(solution)/shard_map/ppermute | solution.py:45
  5.3 1.4 %collective-permute-start.2 = (bf16[256,512]{0,1:T(8,128)(2,1)S(1)}, bf16[256,512]{0,1:T(8,128)(2,1)S(1)}, u32[]{:S(2)}, u32[]{:S(2)}) collective-permute-start(bf16[256,512]{0,1:T(8,128)(2,1)S(1)} %get-tuple-element.6), channel_id=1, source_target_pairs={{0,12},{4,0},{8,4},{12,8},{1,13},{5,1},{9,5},{13,9},{2,14},{6,2},{... | collective-permute-start | bytes 786440 | tf_op jit(solution)/shard_map/ppermute | solution.py:45
  6.7 3.4 %collective-permute-done = bf16[256,512]{0,1:T(8,128)(2,1)S(1)} collective-permute-done((bf16[256,512]{0,1:T(8,128)(2,1)S(1)}, bf16[256,512]{0,1:T(8,128)(2,1)S(1)}, u32[]{:S(2)}, u32[]{:S(2)}) %collective-permute-start) | collective-permute-done | bytes 262176 | tf_op jit(solution)/shard_map/ppermute | solution.py:45
  10.1 15.9 %collective-permute-done.1 = bf16[256,512]{0,1:T(8,128)(2,1)S(1)} collective-permute-done((bf16[256,512]{0,1:T(8,128)(2,1)S(1)}, bf16[256,512]{0,1:T(8,128)(2,1)S(1)}, u32[]{:S(2)}, u32[]{:S(2)}) %collective-permute-start.1) | collective-permute-done | bytes 262176 | tf_op jit(solution)/shard_map/ppermute | solution.py:45
  26.0 2.8 %collective-permute-done.2 = bf16[256,512]{0,1:T(8,128)(2,1)S(1)} collective-permute-done((bf16[256,512]{0,1:T(8,128)(2,1)S(1)}, bf16[256,512]{0,1:T(8,128)(2,1)S(1)}, u32[]{:S(2)}, u32[]{:S(2)}) %collective-permute-start.2) | collective-permute-done | bytes 262176 | tf_op jit(solution)/shard_map/ppermute | solution.py:45
  28.9 0.0 copy-start.1
  28.9 0.0 copy-start.2
  28.9 5.3 %fusion.2 = f32[2048]{0:T(1024)S(1)} fusion(bf16[1,1024,2048]{2,1,0:T(8,128)(2,1)} %param.8, s32[]{:T(128)S(6)} %select_n.61, bf16[1024,512]{0,1:T(8,128)(2,1)S(1)} %constant_dynamic-update-slice_fusion), kind=kOutput, calls=%fused_computation.4 | convolution fusion | flops 2150627328 | bytes 7348228 | tf_op jit(solution)/shard_map/dot_general | solution.py:49
  34.2 0.6 collective-permute-start.3
  34.7 0.8 %collective-permute-done.3 = f32[16,128]{1,0:T(8,128)S(1)} collective-permute-done((f32[16,128]{1,0:T(8,128)S(1)}, f32[16,128]{1,0:T(8,128)S(1)}, u32[]{:S(2)}, u32[]{:S(2)}) %collective-permute-start.3) | collective-permute-done | bytes 8224 | tf_op jit(solution)/shard_map/ppermute | solution.py:60
  35.6 0.3 collective-permute-start.4
  35.8 0.0 copy-done.1
  35.8 0.0 copy-done.2
  35.8 0.2 convolution_bitcast_fusion
  36.0 2.1 %collective-permute-done.4 = f32[16,128]{1,0:T(8,128)S(1)} collective-permute-done((f32[16,128]{1,0:T(8,128)S(1)}, f32[16,128]{1,0:T(8,128)S(1)}, u32[]{:S(2)}, u32[]{:S(2)}) %collective-permute-start.4) | collective-permute-done | bytes 8224 | tf_op jit(solution)/shard_map/ppermute | solution.py:60
  38.1 0.1 subtract_bitcast_fusion
  38.1 5.2 %fusion.25 = (bf16[512,1024]{1,0:T(8,128)(2,1)S(1)}, f32[512,1024]{1,0:T(8,128)S(1)}) fusion(bf16[1,1024,2048]{2,1,0:T(8,128)(2,1)} %param.8, f32[2048]{0:T(1024)S(1)} %subtract_bitcast_fusion, s32[]{:T(128)S(6)} %select_n.61), kind=kOutput, calls=%fused_computation.41 | convolution fusion | flops 2151153664 | bytes 9445380 | tf_op jit(solution)/shard_map/dot_general | solution.py:63
  43.3 0.1 dynamic-slice_bitcast_fusion.2
  43.4 0.1 collective-permute-start.5
  43.5 1.4 %collective-permute-start.6 = (bf16[256,512]{0,1:T(8,128)(2,1)S(1)}, bf16[256,512]{0,1:T(8,128)(2,1)S(1)}, u32[]{:S(2)}, u32[]{:S(2)}) collective-permute-start(bf16[256,512]{0,1:T(8,128)(2,1)S(1)} %get-tuple-element.9), channel_id=1, source_target_pairs={{0,8},{4,12},{8,0},{12,4},{1,9},{5,13},{9,1},{13,5},{2,10},{6,14},... | collective-permute-start | bytes 786440 | tf_op jit(solution)/shard_map/ppermute | solution.py:70
  44.9 1.4 %collective-permute-start.7 = (bf16[256,512]{0,1:T(8,128)(2,1)S(1)}, bf16[256,512]{0,1:T(8,128)(2,1)S(1)}, u32[]{:S(2)}, u32[]{:S(2)}) collective-permute-start(bf16[256,512]{0,1:T(8,128)(2,1)S(1)} %get-tuple-element.8), channel_id=1, source_target_pairs={{0,12},{4,0},{8,4},{12,8},{1,13},{5,1},{9,5},{13,9},{2,14},{6,2},{... | collective-permute-start | bytes 786440 | tf_op jit(solution)/shard_map/ppermute | solution.py:70
  47.0 2.8 %collective-permute-done.5 = bf16[256,512]{0,1:T(8,128)(2,1)S(1)} collective-permute-done((bf16[256,512]{0,1:T(8,128)(2,1)S(1)}, bf16[256,512]{0,1:T(8,128)(2,1)S(1)}, u32[]{:S(2)}, u32[]{:S(2)}) %collective-permute-start.5) | collective-permute-done | bytes 262176 | tf_op jit(solution)/shard_map/ppermute | solution.py:70
  49.8 14.9 %collective-permute-done.6 = bf16[256,512]{0,1:T(8,128)(2,1)S(1)} collective-permute-done((bf16[256,512]{0,1:T(8,128)(2,1)S(1)}, bf16[256,512]{0,1:T(8,128)(2,1)S(1)}, u32[]{:S(2)}, u32[]{:S(2)}) %collective-permute-start.6) | collective-permute-done | bytes 262176 | tf_op jit(solution)/shard_map/ppermute | solution.py:70
  64.7 3.8 %collective-permute-done.7 = bf16[256,512]{0,1:T(8,128)(2,1)S(1)} collective-permute-done((bf16[256,512]{0,1:T(8,128)(2,1)S(1)}, bf16[256,512]{0,1:T(8,128)(2,1)S(1)}, u32[]{:S(2)}, u32[]{:S(2)}) %collective-permute-start.7) | collective-permute-done | bytes 262176 | tf_op jit(solution)/shard_map/ppermute | solution.py:70
  68.5 0.3 fusion.18
  68.9 1.0 %copy.9 = f32[1,256,512]{2,1,0:T(8,128)} copy(f32[1,256,512]{1,2,0:T(8,128)S(1)} %fusion.18) | data formatting | bytes 1048576 | tf_op jit(solution)/shard_map/broadcast_in_dim | solution.py:74
  (8 shorter events, 0.1 us)
Async XLA Ops:
  0.0 0.7 copy-start
  2.8 7.2 %collective-permute-start = (bf16[256,512]{0,1:T(8,128)(2,1)S(1)}, bf16[256,512]{0,1:T(8,128)(2,1)S(1)}, u32[]{:S(2)}, u32[]{:S(2)}) collective-permute-start(bf16[256,512]{0,1:T(8,128)(2,1)S(1)} %get-tuple-element.6), channel_id=1, source_target_pairs={{0,4},{4,8},{8,12},{12,0},{1,5},{5,9},{9,13},{13,1},{2,6},{6,10},{... | collective-permute-start | bytes 786440 | tf_op jit(solution)/shard_map/ppermute | solution.py:45
  4.2 21.8 %collective-permute-start.1 = (bf16[256,512]{0,1:T(8,128)(2,1)S(1)}, bf16[256,512]{0,1:T(8,128)(2,1)S(1)}, u32[]{:S(2)}, u32[]{:S(2)}) collective-permute-start(bf16[256,512]{0,1:T(8,128)(2,1)S(1)} %get-tuple-element.6), channel_id=1, source_target_pairs={{0,8},{4,12},{8,0},{12,4},{1,9},{5,13},{9,1},{13,5},{2,10},{6,14},... | collective-permute-start | bytes 786440 | tf_op jit(solution)/shard_map/ppermute | solution.py:45
  5.3 23.6 %collective-permute-start.2 = (bf16[256,512]{0,1:T(8,128)(2,1)S(1)}, bf16[256,512]{0,1:T(8,128)(2,1)S(1)}, u32[]{:S(2)}, u32[]{:S(2)}) collective-permute-start(bf16[256,512]{0,1:T(8,128)(2,1)S(1)} %get-tuple-element.6), channel_id=1, source_target_pairs={{0,12},{4,0},{8,4},{12,8},{1,13},{5,1},{9,5},{13,9},{2,14},{6,2},{... | collective-permute-start | bytes 786440 | tf_op jit(solution)/shard_map/ppermute | solution.py:45
  28.9 6.9 %copy-start.1 = (s32[16]{0:T(128)S(1)}, s32[16]{0:T(128)}, u32[]{:S(2)}) copy-start(s32[16]{0:T(128)} %param.12) | copy-start | bytes 196
  28.9 6.9 %copy-start.2 = (f32[16]{0:T(128)S(1)}, f32[16]{0:T(128)}, u32[]{:S(2)}) copy-start(f32[16]{0:T(128)} %param.13) | copy-start | bytes 196
  34.2 1.4 %collective-permute-start.3 = (f32[16,128]{1,0:T(8,128)S(1)}, f32[16,128]{1,0:T(8,128)S(1)}, u32[]{:S(2)}, u32[]{:S(2)}) collective-permute-start(f32[16,128]{1,0:T(8,128)S(1)} %bitcast.65), channel_id=1, source_target_pairs={{0,1},{1,0},{2,3},{3,2},{4,5},{5,4},{6,7},{7,6},{8,9},{9,8},{10,11... | collective-permute-start | bytes 24584 | tf_op jit(solution)/shard_map/ppermute | solution.py:60
  35.6 2.5 %collective-permute-start.4 = (f32[16,128]{1,0:T(8,128)S(1)}, f32[16,128]{1,0:T(8,128)S(1)}, u32[]{:S(2)}, u32[]{:S(2)}) collective-permute-start(f32[16,128]{1,0:T(8,128)S(1)} %bitcast_add_fusion.1), channel_id=1, source_target_pairs={{0,2},{2,0},{1,3},{3,1},{4,6},{6,4},{5,7},{7,5},{8,10},{10,8},{9,1... | collective-permute-start | bytes 24584 | tf_op jit(solution)/shard_map/ppermute | solution.py:60
  43.4 6.4 %collective-permute-start.5 = (bf16[256,512]{0,1:T(8,128)(2,1)S(1)}, bf16[256,512]{0,1:T(8,128)(2,1)S(1)}, u32[]{:S(2)}, u32[]{:S(2)}) collective-permute-start(bf16[256,512]{0,1:T(8,128)(2,1)S(1)} %get-tuple-element.7), channel_id=1, source_target_pairs={{0,4},{4,8},{8,12},{12,0},{1,5},{5,9},{9,13},{13,1},{2,6},{6,10},{... | collective-permute-start | bytes 786440 | tf_op jit(solution)/shard_map/ppermute | solution.py:70
  43.5 21.2 %collective-permute-start.6 = (bf16[256,512]{0,1:T(8,128)(2,1)S(1)}, bf16[256,512]{0,1:T(8,128)(2,1)S(1)}, u32[]{:S(2)}, u32[]{:S(2)}) collective-permute-start(bf16[256,512]{0,1:T(8,128)(2,1)S(1)} %get-tuple-element.9), channel_id=1, source_target_pairs={{0,8},{4,12},{8,0},{12,4},{1,9},{5,13},{9,1},{13,5},{2,10},{6,14},... | collective-permute-start | bytes 786440 | tf_op jit(solution)/shard_map/ppermute | solution.py:70
  44.9 23.6 %collective-permute-start.7 = (bf16[256,512]{0,1:T(8,128)(2,1)S(1)}, bf16[256,512]{0,1:T(8,128)(2,1)S(1)}, u32[]{:S(2)}, u32[]{:S(2)}) collective-permute-start(bf16[256,512]{0,1:T(8,128)(2,1)S(1)} %get-tuple-element.8), channel_id=1, source_target_pairs={{0,12},{4,0},{8,4},{12,8},{1,13},{5,1},{9,5},{13,9},{2,14},{6,2},{... | collective-permute-start | bytes 786440 | tf_op jit(solution)/shard_map/ppermute | solution.py:70
